TPU v7x, 32 devices: a whole 2x2x4 slice. The times are simulated.
32 devices in a mesh: freq: 2 (over y), blk: 8 (over z, x), line: 2 (over core).
Axes of the slice: x: 2, y: 2, z: 4, core: 2. Of those that a mesh axis runs over, the one named last changes fastest.
Arguments:
- base_state: float32 [2, 5, 512, 16, 256], P(None, None, ('freq', 'blk'), None, 'line'), parts along dimension 2, may hold values from -6 to 6
- gust_source: float32 [2, 5, 512, 16, 256], P(None, None, ('freq', 'blk'), None, 'line'), parts along dimension 2, may hold values from -6 to 6
- frequency: float32 [2], P('freq'), parts along dimension 0, may hold values from 0.5 to 3
- jacobians: float32 [8, 3, 5, 5], P('blk'), may hold values from -2.5 to 2.5
- dissipation: float32 [256, 16, 256], P('blk', None, 'line'), may hold values from 0.01 to 0.08
- time_step: float32 [256, 16, 256], P('blk', None, 'line'), may hold values from 0.1 to 1
- line_inverse: float32 [16, 256, 256], replicated, may hold values from 0 to 1
- orientation: int32 [8, 2], P('blk'), may hold values from 0 to 1, as said below
Outputs:
- section_state: float32 [2, 5, 512, 16, 256], P(None, None, ('freq', 'blk'), None, 'line'), parts along dimension 2
- smoothed_residual: float32 [2, 5, 512, 16, 256], P(None, None, ('freq', 'blk'), None, 'line'), parts along dimension 2
There are 2 independent parts, one for each index of `freq`. A program takes and returns all parts, laid end to end along the dimension named above; an argument that names none is the same for every part. Nothing has to cross between parts.
Inputs may be any that keep to these rules, and one draw needn't show every extreme that they name: `orientation`: entry [b, 1] equals entry [(b + 1) mod 8, 0]: both describe the same face.
All inputs are finite; a program needn't handle non-finite values.
Results may differ from a plain program's by a relative error of at most 0.0003.
Values sent between devices are 32-bit elements; how exact they have to be, the bound alone decides.
A program may use at most 128 MiB of HBM per device.

v0:
```python
import jax
import jax.numpy as jnp
from jax import lax
from jax.sharding import PartitionSpec as P

highest = lax.Precision.HIGHEST
section_coefficient = 0.25


def extended(block, sides, width):
    for axis, dim in sides:
        count = lax.axis_size(axis)
        forward = [(i, i + 1) for i in range(count - 1)]
        forward.append((count - 1, 0))
        backward = [(target, source) for source, target in forward]
        low = lax.ppermute(
            lax.slice_in_dim(block, block.shape[dim] - width, None, axis=dim), axis, forward
        )
        high = lax.ppermute(lax.slice_in_dim(block, 0, width, axis=dim), axis, backward)
        block = jnp.concatenate([low, block, high], axis=dim)
    return block


def reorient(planes, facing):
    variable_index = lax.broadcasted_iota(jnp.int32, (1, planes.shape[1], 1, 1, 1), 1)
    sign_row = jnp.where(variable_index == 2, -1.0, 1.0).astype(planes.dtype)
    turned = planes[:, :, :, ::-1, :] * sign_row
    return jnp.where(facing == 1, turned, planes)


def direction_terms(padded, dimension, length, jacobian, damping):

    def shifted(offset):
        return lax.slice_in_dim(padded, offset, offset + length, axis=dimension)

    back_two, back_one, centre, ahead_one, ahead_two = (
        shifted(0),
        shifted(1),
        shifted(2),
        shifted(3),
        shifted(4),
    )
    central = 0.5 * (ahead_one - back_one)
    convected = jnp.einsum("vw,cwkja->cvkja", jacobian, central, precision=highest)
    fourth = ahead_two - 4.0 * ahead_one + 6.0 * centre - 4.0 * back_one + back_two
    return convected + damping * fourth


def section_residual(fields, kpadded, ipadded, jacobian, damping, source, omega_value):
    jpadded = jnp.pad(fields, ((0, 0), (0, 0), (0, 0), (2, 2), (0, 0)))
    summed = direction_terms(ipadded, 4, fields.shape[4], jacobian[0], damping)
    summed = summed + direction_terms(jpadded, 3, fields.shape[3], jacobian[1], damping)
    summed = summed + direction_terms(kpadded, 2, fields.shape[2], jacobian[2], damping)
    rotated = jnp.stack([-omega_value * fields[1], omega_value * fields[0]])
    return summed + rotated - source


def body(
    base_state, gust_source, frequency, jacobians, dissipation, time_step, line_inverse, orientation
):
    facing = orientation[0]
    kpadded = extended(base_state, (("blk", 2),), 2)
    ipadded = extended(base_state, (("line", 4),), 2)
    planes_total = kpadded.shape[2]
    kpadded = jnp.concatenate(
        [
            reorient(kpadded[:, :, :2], facing[0]),
            kpadded[:, :, 2 : planes_total - 2],
            reorient(kpadded[:, :, planes_total - 2 :], facing[1]),
        ],
        axis=2,
    )
    residual = section_residual(
        base_state, kpadded, ipadded, jacobians[0], dissipation, gust_source, frequency[0]
    )
    line_rows = base_state.shape[4]
    column = lax.axis_index("line")
    own_rows = lax.dynamic_slice_in_dim(line_inverse, column * line_rows, line_rows, 1)
    smoothed = jnp.einsum(
        "jab,cvkjb->cvkja",
        own_rows,
        lax.all_gather(residual, "line", axis=4, tiled=True),
        precision=highest,
    )
    advanced = base_state - section_coefficient * time_step * smoothed
    return (advanced, smoothed)


def solution(mesh):
    in_specs = (
        P(None, None, ("freq", "blk"), None, "line"),
        P(None, None, ("freq", "blk"), None, "line"),
        P("freq"),
        P("blk", None, None, None),
        P("blk", None, "line"),
        P("blk", None, "line"),
        P(),
        P("blk", None),
    )
    out_specs = (
        P(None, None, ("freq", "blk"), None, "line"),
        P(None, None, ("freq", "blk"), None, "line"),
    )
    return jax.shard_map(body, mesh=mesh, in_specs=in_specs, out_specs=out_specs, check_vma=False)
```

profile of v0, /device:TPU:0, one launch (start us, length us, event | category | flops | bytes accessed | tf_op | source)
XLA Modules:
  0.0 114.4 jit_solution(13213371524876990866)
XLA Ops:
  7.2 0.0 all-gather.2.cloned.1.call-start
  7.2 0.0 copy-start
  7.2 2.7 %copy.51 = f32[2,5,32,16,128]{4,2,1,0,3:T(8,128)S(1)} copy(f32[2,5,32,16,128]{4,3,2,1,0:T(8,128)} %param.8) | data formatting | bytes 5242880 | tf_op args[0]
  10.0 0.1 fusion.39
  10.1 6.0 %collective-permute-start.2 = (f32[2,5,2,16,128]{4,2,1,0,3:T(2,128)S(1)}, f32[2,5,2,16,128]{4,2,1,0,3:T(2,128)S(1)}, u32[]{:S(2)}, u32[]{:S(2)}) collective-permute-start(f32[2,5,2,16,128]{4,2,1,0,3:T(2,128)S(1)} %get-tuple-element.13), channel_id=1, source_target_pairs={{2,0},{4,2},{6,4},{8,6},{10,8},{12,10},{14,12},{0,14},{3,1},{5,3},... | collective-permute-start | bytes 491528 | tf_op jit(solution)/shard_map/ppermute | solution.py:19
  16.1 3.2 %fusion.38 = (f32[2,5,32,16,2]{4,3,2,1,0:T(8,128)}, f32[2,5,32,16,2]{4,3,2,1,0:T(8,128)}) fusion(f32[2,5,32,16,128]{4,3,2,1,0:T(8,128)S(1)} %copy-done), kind=kLoop, calls=%fused_computation.66 | loop fusion | bytes 163840 | tf_op jit(solution)/shard_map/slice | solution.py:19
  19.3 2.8 %copy.64 = f32[2,5,32,16,2]{2,3,4,1,0:T(8,128)S(1)} copy(f32[2,5,32,16,2]{4,3,2,1,0:T(8,128)} %get-tuple-element.11) | data formatting | bytes 81920
  22.2 0.1 collective-permute-start
  22.2 3.5 %copy.65 = f32[2,5,32,16,2]{2,3,4,1,0:T(8,128)} copy(f32[2,5,32,16,2]{4,3,2,1,0:T(8,128)} %get-tuple-element.12) | data formatting | bytes 81920
  25.7 0.5 collective-permute-start.1
  26.9 0.0 copy-start.7
  26.9 0.0 copy-start.4
  26.9 1.9 %slice_multiply_fusion.1 = (f32[1,5,32,16,128]{4,2,1,0,3:T(8,128)}, f32[1,5,32,16,128]{4,2,1,0,3:T(8,128)}) fusion(f32[2,5,32,16,128]{4,2,1,0,3:T(8,128)S(1)} %copy.51, f32[]{:T(128)S(6)} %neg.3, f32[]{:T(128)} %bitcast.43), kind=kLoop, calls=%fused_computation.57 | loop fusion | flops 655360 | bytes 5242888 | tf_op jit(solution)/shard_map/mul | solution.py:54
  28.8 0.6 fusion.41
  30.6 0.8 copy.39
  31.4 3.4 %copy.34 = f32[2,5,32,16,2]{4,2,1,0,3:T(8,128)} copy(f32[2,5,32,16,2]{2,3,4,1,0:T(8,128)} %collective-permute-done) | data formatting | bytes 81920 | tf_op jit(solution)/shard_map/ppermute | solution.py:19
  34.9 3.4 %copy.36 = f32[2,5,32,16,2]{4,2,1,0,3:T(8,128)} copy(f32[2,5,32,16,2]{2,3,4,1,0:T(8,128)} %collective-permute-done.1) | data formatting | bytes 81920 | tf_op jit(solution)/shard_map/ppermute | solution.py:16
  38.3 0.7 copy-done.5
  38.9 1.2 %multiply_select_fusion.1 = (f32[2,5,2,16,128]{4,2,1,0,3:T(2,128)S(1)}, f32[2,5,2,16,128]{4,2,1,0,3:T(2,128)S(1)}) fusion(f32[2,5,2,16,128]{4,2,1,0,3:T(2,128)S(1)} %collective-permute-done.2, pred[]{:T(512)} %bitcast.8, f32[5]{0:T(128)S(1)} %compare_select_fusion, f32[2,5,2,16,128]{4,2,1,0,3:T(2,128)} %copy-done.5, pred[]{:T(512)} %bitcast.9), kind=kLoop, calls=%fused_computation.59 | loop fusion | flops 163840 | bytes 655382 | tf_op jit(solution)/shard_map/jit(_where)/select_n | solution.py:28
  40.1 6.2 %subtract_multiply_fusion.2 = (f32[2,5,32,16,128]{4,2,1,0,3:T(8,128)S(1)}, f32[2,5,32,16,128]{4,2,1,0,3:T(8,128)S(1)}, f32[2,5,32,16,128]{4,2,1,0,3:T(8,128)S(1)}) fusion(f32[2,5,32,16,2]{4,2,1,0,3:T(8,128)} %copy.34, f32[2,5,32,16,128]{4,2,1,0,3:T(8,128)S(1)} %copy.51, f32[2,5,32,16,2]{4,2,1,0,3:T(8,128)} %copy.36, ...), kind=kLoop, calls=%fused_computation.51 | loop fusion | flops 6553600 | bytes 10895360 | tf_op jit(solution)/shard_map/mul | solution.py:43
  46.3 6.0 %fusion = f32[2,32,16,128,5]{3,4,2,1,0:T(8,128)S(1)} fusion(f32[2,5,32,16,128]{4,2,1,0,3:T(8,128)S(1)} %get-tuple-element.7, f32[1,1,5,5]{3,0,2,1:T(1,128)S(1)} %get-tuple-element.17), kind=kOutput, calls=%fused_computation.4 | convolution fusion | flops 39321600 | bytes 5242980 | tf_op jit(solution)/shard_map/vw,cwkja->cvkja/dot_general | solution.py:44
  52.4 6.0 %fusion.2 = f32[2,32,16,128,5]{3,4,2,1,0:T(8,128)S(1)} fusion(f32[2,5,32,16,128]{4,2,1,0,3:T(8,128)S(1)} %get-tuple-element.8, f32[1,1,5,5]{3,0,2,1:T(1,128)S(1)} %get-tuple-element.16), kind=kOutput, calls=%fused_computation.6 | convolution fusion | flops 39321600 | bytes 5242980 | tf_op jit(solution)/shard_map/vw,cwkja->cvkja/dot_general | solution.py:44
  58.4 0.0 copy-start.3
  58.4 6.2 %fusion.4 = f32[2,32,16,128,5]{3,4,2,1,0:T(8,128)S(1)} fusion(f32[2,5,32,16,128]{4,2,1,0,3:T(8,128)S(1)} %get-tuple-element.6, f32[1,1,5,5]{3,0,2,1:T(1,128)S(1)} %get-tuple-element.15), kind=kOutput, calls=%fused_computation.8 | convolution fusion | flops 39321600 | bytes 5242980 | tf_op jit(solution)/shard_map/vw,cwkja->cvkja/dot_general | solution.py:44
  64.7 11.5 %fusion.17 = f32[2,5,32,16,128]{4,2,1,0,3:T(8,128)} fusion(f32[2,5,32,16,128]{4,2,1,0,3:T(8,128)S(1)} %copy.51, f32[2,5,2,16,128]{4,2,1,0,3:T(2,128)S(1)} %get-tuple-element.19, f32[2,5,2,16,128]{4,2,1,0,3:T(2,128)S(1)} %get-tuple-element.18, f32[2,5,32,16,2]{4,2,1,0,3:T(8,128)S(1)} %copy-done.3, f32[2,5,32,16,2]{4,2,1,0,3:T(8,128)S(1)} %copy-done.2, ...), kind=kLoop, calls=%fused_computation.29 | loop fusion | flops 24903680 | bytes 19021824 | tf_op jit(solution)/shard_map/sub | solution.py:55
  76.2 0.0 all-gather.2.cloned.1.call-update
  76.2 1.1 broadcast_multiply_fusion
  77.3 0.1 copy.31
  77.4 14.7 %all-gather.2.cloned.1.call-done = f32[2,5,32,16,256]{4,2,1,0,3:T(8,128)} async-done(((f32[2,5,32,16,128]{4,2,1,0,3:T(8,128)}), f32[2,5,32,16,256]{4,2,1,0,3:T(8,128)}) %all-gather.2.cloned.1.call-update) | async-done | bytes 5242896 | tf_op jit(solution)/shard_map/all_gather | solution.py:82
  92.1 9.2 %multiply_subtract_fusion = (f32[2,5,32,16,128]{4,2,1,0,3:T(8,128)S(1)}, f32[2,5,32,16,128]{4,2,1,0,3:T(8,128)S(1)}) fusion(f32[32,16,128]{2,0,1:T(8,128)S(1)} %copy.31, f32[2,5,32,16,128]{4,3,2,1,0:T(8,128)S(1)} %copy-done.1, f32[2,5,32,16,256]{4,2,1,0,3:T(8,128)} %all-gather.2.cloned.1.call-done, f32[16,256,256]{2,1,0:T(8,128)} %param.14, s32[]{:T(128)S(6)} %select_n.34), kind=kOutput, calls=%fused_computation.48 | convolution fusion | flops 2014576640 | bytes 15466500 | tf_op jit(solution)/shard_map/jab,cvkjb->cvkja/dot_general | solution.py:79
  101.3 3.1 %copy.52 = f32[2,5,32,16,128]{4,3,2,1,0:T(8,128)} copy(f32[2,5,32,16,128]{4,2,1,0,3:T(8,128)S(1)} %get-tuple-element.22) | data formatting | bytes 5242880
  104.4 3.1 %copy.53 = f32[2,5,32,16,128]{4,3,2,1,0:T(8,128)} copy(f32[2,5,32,16,128]{4,2,1,0,3:T(8,128)S(1)} %get-tuple-element.23) | data formatting | bytes 5242880
  (18 shorter events, 0.0 us)
Async XLA Ops:
  7.2 84.9 %all-gather.2.cloned.1.call-start = ((), (), s32[]{:S(2)}) async-start(), calls=%async_computation | async-start | bytes 7864320 | tf_op jit(solution)/shard_map/all_gather | solution.py:82
  7.2 8.9 %copy-start = (f32[2,5,32,16,128]{4,3,2,1,0:T(8,128)S(1)}, f32[2,5,32,16,128]{4,3,2,1,0:T(8,128)}, u32[]{:S(2)}) copy-start(f32[2,5,32,16,128]{4,3,2,1,0:T(8,128)} %param.8) | copy-start | bytes 7864324
  10.1 28.2 %collective-permute-start.2 = (f32[2,5,2,16,128]{4,2,1,0,3:T(2,128)S(1)}, f32[2,5,2,16,128]{4,2,1,0,3:T(2,128)S(1)}, u32[]{:S(2)}, u32[]{:S(2)}) collective-permute-start(f32[2,5,2,16,128]{4,2,1,0,3:T(2,128)S(1)} %get-tuple-element.13), channel_id=1, source_target_pairs={{2,0},{4,2},{6,4},{8,6},{10,8},{12,10},{14,12},{0,14},{3,1},{5,3},... | collective-permute-start | bytes 491528 | tf_op jit(solution)/shard_map/ppermute | solution.py:19
  16.1 22.2 %collective-permute-start.3 = (f32[2,5,2,16,128]{4,2,1,0,3:T(2,128)S(1)}, f32[2,5,2,16,128]{4,2,1,0,3:T(2,128)S(1)}, u32[]{:S(2)}, u32[]{:S(2)}) collective-permute-start(f32[2,5,2,16,128]{4,2,1,0,3:T(2,128)S(1)} %get-tuple-element.14), channel_id=1, source_target_pairs={{0,2},{2,4},{4,6},{6,8},{8,10},{10,12},{12,14},{14,0},{1,3},{3,5},... | collective-permute-start | bytes 491528 | tf_op jit(solution)/shard_map/ppermute | solution.py:16
  19.3 6.9 %copy-start.6 = (f32[1,3,5,5]{3,0,2,1:T(1,128)S(1)}, f32[1,3,5,5]{3,0,2,1:T(1,128)}, u32[]{:S(2)}) copy-start(f32[1,3,5,5]{3,0,2,1:T(1,128)} %param.11) | copy-start | bytes 904
  22.2 9.3 %collective-permute-start = (f32[2,5,32,16,2]{2,3,4,1,0:T(8,128)S(1)}, f32[2,5,32,16,2]{2,3,4,1,0:T(8,128)}, u32[]{:S(2)}, u32[]{:S(2)}) collective-permute-start(f32[2,5,32,16,2]{2,3,4,1,0:T(8,128)S(1)} %copy.64), channel_id=1, source_target_pairs={{1,0},{0,1},{3,2},{2,3},{5,4},{4,5},{7,6},{6,7},{9,8},{8,9},{11,10... | collective-permute-start | bytes 122888 | tf_op jit(solution)/shard_map/ppermute | solution.py:19
  25.7 9.1 %collective-permute-start.1 = (f32[2,5,32,16,2]{2,3,4,1,0:T(8,128)}, f32[2,5,32,16,2]{2,3,4,1,0:T(8,128)}, u32[]{:S(2)}, u32[]{:S(2)}) collective-permute-start(f32[2,5,32,16,2]{2,3,4,1,0:T(8,128)} %copy.65), channel_id=1, source_target_pairs={{0,1},{1,0},{2,3},{3,2},{4,5},{5,4},{6,7},{7,6},{8,9},{9,8},{10,11... | collective-permute-start | bytes 122888 | tf_op jit(solution)/shard_map/ppermute | solution.py:16
  26.9 1.9 %copy-start.7 = (s32[1,2]{1,0:T(1,128)S(1)}, s32[1,2]{1,0:T(1,128)}, u32[]{:S(2)}) copy-start(s32[1,2]{1,0:T(1,128)} %param.15) | copy-start | bytes 28
  26.9 3.7 %copy-start.4 = (f32[32,16,128]{2,1,0:T(8,128)S(1)}, f32[32,16,128]{2,1,0:T(8,128)}, u32[]{:S(2)}) copy-start(f32[32,16,128]{2,1,0:T(8,128)} %param.12) | copy-start | bytes 786436
  38.3 0.7 copy-start.5
  58.4 6.3 %copy-start.2 = (f32[2,5,32,16,2]{4,2,1,0,3:T(8,128)S(1)}, f32[2,5,32,16,2]{4,2,1,0,3:T(8,128)}, u32[]{:S(2)}) copy-start(f32[2,5,32,16,2]{4,2,1,0,3:T(8,128)} %copy.34) | copy-start | bytes 122884
  58.4 6.3 %copy-start.3 = (f32[2,5,32,16,2]{4,2,1,0,3:T(8,128)S(1)}, f32[2,5,32,16,2]{4,2,1,0,3:T(8,128)}, u32[]{:S(2)}) copy-start(f32[2,5,32,16,2]{4,2,1,0,3:T(8,128)} %copy.36) | copy-start | bytes 122884
  76.2 15.9 %copy-start.1 = (f32[2,5,32,16,128]{4,3,2,1,0:T(8,128)S(1)}, f32[2,5,32,16,128]{4,3,2,1,0:T(8,128)}, u32[]{:S(2)}) copy-start(f32[2,5,32,16,128]{4,3,2,1,0:T(8,128)} %param.8) | copy-start | bytes 7864324
Sparse Core Ops, SparseCore 0:
  76.3 15.7 all-gather.1
where the time goes:
time: 115 us; the launch traced here: 114 us
  local copies, waits for them, and re-layouts  27.6 us (24%)
  matrix products  27.5 us (24%)
  other arithmetic  21.8 us (19%)
  between operations  16.1 us (14%)
  waiting for transfers between devices  14.7 us (13%)
  starting transfers between devices  6.61 us (6%)
    dot_general x3, matrix products, direction_terms(): jnp.einsum('vw,cwkja->cvkja', jacobian, central, precision=highest)  18.3 us
    unnamed x22, local copies, waits for them, and re-layouts  16.8 us
    all_gather x1, waiting for transfers between devices, body(): lax.all_gather(residual, 'line', axis=4, tiled=True)  14.7 us
    sub x1, other arithmetic, section_residual(): return summed + rotated - source  11.5 us
    dot_general x1, matrix products, body(): jnp.einsum('jab,cvkjb->cvkja', own_rows, lax.all_gather(residual, 'line',...  9.21 us
    mul x1, other arithmetic, direction_terms(): central = 0.5 * (ahead_one - back_one)  6.18 us
    ppermute x2, starting transfers between devices, extended(): lax.ppermute(lax.slice_in_dim(block, 0, width, axis=dim), axis, backward)  6.08 us
    ppermute x1, local copies, waits for them, and re-layouts, extended(): lax.ppermute(lax.slice_in_dim(block, block.shape[dim] - width, None, axis...  3.41 us
  transfers between devices with their start and end apart: 5, of which 1 were waited for; matrix products, arithmetic and copies ran while one was open for 18% of the time, Pallas kernels for 0%

commit v1 on v0

v1 whole, which is shorter than its diff:
```python
import functools

import jax
import jax.numpy as jnp
from jax import lax
from jax.experimental import pallas as pl
from jax.experimental.pallas import tpu as pltpu
from jax.sharding import PartitionSpec as P

MESH = pl.DeviceIdType.MESH
section_coefficient = 0.25
PAIR = 2


def kernel(
    sizes,
    jac,
    freq,
    facing,
    base,
    gust,
    damp,
    step,
    inverse,
    advanced,
    smoothed,
    ubuf,
    gbuf,
    dbuf,
    tbuf,
    wbuf,
    wcat,
    pack_out,
    pack_in,
    own,
    other,
    turned,
    local_sem,
    halo_send,
    halo_recv,
    pack_send,
    pack_recv,
    res_send,
    res_recv,
):
    nblk, kl, nj, ni, cv = sizes
    nv = cv // 2
    f32, bf16 = jnp.float32, jnp.bfloat16
    blk = lax.axis_index("blk")
    line = lax.axis_index("line")
    right = lax.rem(blk + 1, nblk)
    left = lax.rem(blk + nblk - 1, nblk)
    mate = 1 - line

    loads = [
        pltpu.make_async_copy(
            base, ubuf.at[:, pl.ds(2, kl), pl.ds(8, nj), :], local_sem.at[0]
        ),
        pltpu.make_async_copy(
            inverse.at[:, pl.ds(pl.multiple_of(line * ni, ni), ni), pl.ds(pl.multiple_of(line * ni, ni), ni)],
            wbuf.at[:, :, pl.ds(0, ni)],
            local_sem.at[1],
        ),
        pltpu.make_async_copy(
            inverse.at[:, pl.ds(pl.multiple_of(line * ni, ni), ni), pl.ds(pl.multiple_of(mate * ni, ni), ni)],
            wbuf.at[:, :, pl.ds(ni, ni)],
            local_sem.at[2],
        ),
        pltpu.make_async_copy(gust, gbuf, local_sem.at[3]),
        pltpu.make_async_copy(damp, dbuf, local_sem.at[4]),
        pltpu.make_async_copy(step, tbuf, local_sem.at[5]),
    ]
    for copy in loads:
        copy.start()

    barrier = pltpu.get_barrier_semaphore()
    pl.semaphore_signal(barrier, inc=1, device_id={"blk": right}, device_id_type=MESH)
    pl.semaphore_signal(barrier, inc=1, device_id={"blk": left}, device_id_type=MESH)
    pl.semaphore_signal(barrier, inc=1, device_id={"line": mate}, device_id_type=MESH)
    pl.semaphore_wait(barrier, 3)

    to_right = pltpu.make_async_remote_copy(
        src_ref=base.at[:, pl.ds(kl - 2, 2)],
        dst_ref=ubuf.at[:, pl.ds(0, 2), pl.ds(8, nj), :],
        send_sem=halo_send.at[0],
        recv_sem=halo_recv.at[0],
        device_id={"blk": right},
        device_id_type=MESH,
    )
    to_left = pltpu.make_async_remote_copy(
        src_ref=base.at[:, pl.ds(0, 2)],
        dst_ref=ubuf.at[:, pl.ds(kl + 2, 2), pl.ds(8, nj), :],
        send_sem=halo_send.at[1],
        recv_sem=halo_recv.at[1],
        device_id={"blk": left},
        device_id_type=MESH,
    )
    to_right.start()
    to_left.start()

    def clear(k, carry):
        zero = jnp.zeros((cv, 8, ni), f32)
        ubuf[:, k + 2, 0:8, :] = zero
        ubuf[:, k + 2, nj + 8 : nj + 16, :] = zero
        return carry

    lax.fori_loop(0, kl, clear, 0)

    lane = lax.broadcasted_iota(jnp.int32, (nj, ni), 1)
    edge = (lane < 2) | (lane >= ni - 2)

    loads[0].wait()

    def pack(k, carry):
        return tuple(
            carry[n]
            + pltpu.roll(jnp.where(edge, ubuf[n, k + 2, 8 : nj + 8, :], 0.0), 4 * k, 1)
            for n in range(cv)
        )

    packed = lax.fori_loop(
        0, kl, pack, tuple(jnp.zeros((nj, ni), f32) for _ in range(cv))
    )
    for n in range(cv):
        pack_out[n] = packed[n]
    swap = pltpu.make_async_remote_copy(
        src_ref=pack_out,
        dst_ref=pack_in,
        send_sem=pack_send,
        recv_sem=pack_recv,
        device_id={"line": mate},
        device_id_type=MESH,
    )
    swap.start()

    loads[1].wait()
    loads[2].wait()

    def split(j, carry):
        values = wbuf[j]
        high = values.astype(bf16)
        wcat[j, 0:ni, :] = high
        wcat[j, ni : 2 * ni, :] = (values - high.astype(f32)).astype(bf16)
        return carry

    lax.fori_loop(0, nj, split, 0)

    loads[3].wait()
    loads[4].wait()
    loads[5].wait()
    swap.wait()

    omega = freq[0]

    def plane(k):
        damping = dbuf[k]
        shift = lax.rem(ni - 4 * k, ni)
        for c in range(2):
            central = []
            fourth = []
            for v in range(nv):
                n = c * nv + v
                u = ubuf[n, k + 2, 8 : nj + 8, :]
                k1, k2 = ubuf[n, k + 3, 8 : nj + 8, :], ubuf[n, k + 4, 8 : nj + 8, :]
                kb1, kb2 = ubuf[n, k + 1, 8 : nj + 8, :], ubuf[n, k, 8 : nj + 8, :]
                j1, j2 = ubuf[n, k + 2, 9 : nj + 9, :], ubuf[n, k + 2, 10 : nj + 10, :]
                jb1, jb2 = ubuf[n, k + 2, 7 : nj + 7, :], ubuf[n, k + 2, 6 : nj + 6, :]
                h = pltpu.roll(pack_in[n], shift, 1)
                i1 = pltpu.roll(jnp.where(lane == 0, h, u), ni - 1, 1)
                i2 = pltpu.roll(jnp.where(lane < 2, h, u), ni - 2, 1)
                ib1 = pltpu.roll(jnp.where(lane == ni - 1, h, u), 1, 1)
                ib2 = pltpu.roll(jnp.where(lane >= ni - 2, h, u), 2, 1)
                central.append((i1 - ib1, j1 - jb1, k1 - kb1))
                fourth.append(
                    ((k2 + kb2) + (j2 + jb2) + (i2 + ib2))
                    - 4.0 * ((k1 + kb1) + (j1 + jb1) + (i1 + ib1))
                    + 18.0 * u
                )
            for v in range(nv):
                total = damping * fourth[v] - gbuf[c * nv + v, k]
                if c == 0:
                    total = total - omega * ubuf[nv + v, k + 2, 8 : nj + 8, :]
                else:
                    total = total + omega * ubuf[v, k + 2, 8 : nj + 8, :]
                for w in range(nv):
                    for d in range(3):
                        total = total + jac[d * nv * nv + v * nv + w] * central[w][d]
                own[c * nv + v, pl.ds(pl.multiple_of(k * nj, nj), nj), :] = total

    def send(pair):
        rows = pl.ds(pl.multiple_of(pair * (PAIR * nj), PAIR * nj), PAIR * nj)
        return pltpu.make_async_remote_copy(
            src_ref=own.at[:, rows, :],
            dst_ref=other.at[:, rows, :],
            send_sem=res_send.at[pair],
            recv_sem=res_recv.at[pair],
            device_id={"line": mate},
            device_id_type=MESH,
        )

    def work(pair):
        def one(k, carry):
            plane(pair * PAIR + k)
            return carry

        lax.fori_loop(0, PAIR, one, 0)
        send(pair).start()

    pairs = kl // PAIR
    quarter = pairs // 4

    def middle_pair(n):
        return n + quarter

    def outer_pair(n):
        return n + 1 + (n // (quarter - 1)) * (pairs // 2)

    def run_middle(n, carry):
        work(middle_pair(n))
        return carry

    def run_outer(n, carry):
        work(outer_pair(n))
        return carry

    lax.fori_loop(0, pairs // 2, run_middle, 0)
    lax.fori_loop(0, 2 * (quarter - 1), run_outer, 0)

    def product(starts, count):
        def one(j, carry):
            mine, theirs = [], []
            for n in range(cv):
                for k0 in starts:
                    rows = pl.ds(k0 * nj + j, count, stride=nj)
                    mine.append(own[n, rows, :])
                    theirs.append(other[n, rows, :])
            x = jnp.concatenate(
                [jnp.concatenate(mine, axis=0), jnp.concatenate(theirs, axis=0)], axis=1
            )
            high = x.astype(bf16)
            low = (x - high.astype(f32)).astype(bf16)
            weight = wcat[j]
            contract = (((1,), (1,)), ((), ()))
            both = lax.dot_general(high, weight, contract, preferred_element_type=f32)
            rest = lax.dot_general(
                low, weight[0:ni], contract, preferred_element_type=f32
            )
            out = both[:, 0:ni] + (both[:, ni : 2 * ni] + rest)
            at = 0
            for n in range(cv):
                for k0 in starts:
                    smoothed[n, pl.ds(k0 * nj + j, count, stride=nj), :] = out[
                        at : at + count
                    ]
                    at += count
            return carry

        lax.fori_loop(0, nj, one, 0)

    def update(first, number):
        def one(k, carry):
            rows = pl.ds(pl.multiple_of((first + k) * nj, nj), nj)
            scale = section_coefficient * tbuf[first + k]
            for n in range(cv):
                advanced[n, rows, :] = (
                    ubuf[n, first + k + 2, 8 : nj + 8, :] - scale * smoothed[n, rows, :]
                )
            return carry

        lax.fori_loop(0, number, one, 0)

    def arrived(n, carry):
        send(middle_pair(n)).wait_recv()
        return carry

    lax.fori_loop(0, pairs // 2, arrived, 0)
    product([kl // 4], kl // 2)
    update(kl // 4, kl // 2)

    to_right.wait()
    to_left.wait()

    for side, first in ((0, 0), (1, kl + 2)):
        turn = facing[side] == 1
        for p in range(2):
            for n in range(cv):
                turned[n * 2 + p] = ubuf[n, first + p, 8 : nj + 8, :]
        for p in range(2):
            for n in range(cv):
                sign = -1.0 if n % nv == 2 else 1.0
                rows = [turned[n * 2 + p, r : r + 1, :] for r in range(nj - 1, -1, -1)]
                flipped = sign * jnp.concatenate(rows, axis=0)
                ubuf[n, first + p, 8 : nj + 8, :] = jnp.where(
                    turn, flipped, turned[n * 2 + p]
                )

    work(0)
    work(pairs - 1)

    def outer_arrived(n, carry):
        send(outer_pair(n)).wait_recv()
        return carry

    lax.fori_loop(0, 2 * (quarter - 1), outer_arrived, 0)
    send(0).wait_recv()
    send(pairs - 1).wait_recv()
    product([0, kl - kl // 4], kl // 4)
    update(0, kl // 4)
    update(kl - kl // 4, kl // 4)

    def sent(pair, carry):
        send(pair).wait_send()
        return carry

    lax.fori_loop(0, pairs, sent, 0)


def body(
    nblk,
    base_state,
    gust_source,
    frequency,
    jacobians,
    dissipation,
    time_step,
    line_inverse,
    orientation,
):
    nc, nv, kl, nj, ni = base_state.shape
    cv = nc * nv
    f32 = jnp.float32
    pairs = kl // PAIR
    out = pltpu.VMEM((cv, kl * nj, ni), f32)
    smem = pl.BlockSpec(memory_space=pltpu.SMEM)
    hbm = pl.BlockSpec(memory_space=pltpu.HBM)
    vmem = pl.BlockSpec(memory_space=pltpu.VMEM)
    dma = pltpu.SemaphoreType.DMA
    advanced, smoothed = pl.pallas_call(
        functools.partial(kernel, (nblk, kl, nj, ni, cv)),
        out_shape=(out, out),
        in_specs=[smem] * 3 + [hbm] * 5,
        out_specs=(vmem, vmem),
        scratch_shapes=[
            pltpu.VMEM((cv, kl + 4, nj + 16, ni), f32),
            pltpu.VMEM((cv, kl, nj, ni), f32),
            pltpu.VMEM((kl, nj, ni), f32),
            pltpu.VMEM((kl, nj, ni), f32),
            pltpu.VMEM((nj, ni, 2 * ni), f32),
            pltpu.VMEM((nj, 2 * ni, 2 * ni), jnp.bfloat16),
            pltpu.VMEM((cv, nj, ni), f32),
            pltpu.VMEM((cv, nj, ni), f32),
            pltpu.VMEM((cv, kl * nj, ni), f32),
            pltpu.VMEM((cv, kl * nj, ni), f32),
            pltpu.VMEM((cv * 2, nj, ni), f32),
            dma((6,)),
            dma((2,)),
            dma((2,)),
            dma,
            dma,
            dma((pairs,)),
            dma((pairs,)),
        ],
        compiler_params=pltpu.CompilerParams(
            collective_id=0, has_side_effects=True, vmem_limit_bytes=54 * 1024 * 1024
        ),
    )(
        0.5 * jacobians.reshape(-1),
        frequency,
        orientation.reshape(-1),
        base_state.reshape(cv, kl, nj, ni),
        gust_source.reshape(cv, kl, nj, ni),
        dissipation,
        time_step,
        line_inverse,
    )
    return advanced.reshape(base_state.shape), smoothed.reshape(base_state.shape)


def solution(mesh):
    in_specs = (
        P(None, None, ("freq", "blk"), None, "line"),
        P(None, None, ("freq", "blk"), None, "line"),
        P("freq"),
        P("blk", None, None, None),
        P("blk", None, "line"),
        P("blk", None, "line"),
        P(),
        P("blk", None),
    )
    out_specs = (
        P(None, None, ("freq", "blk"), None, "line"),
        P(None, None, ("freq", "blk"), None, "line"),
    )
    return jax.shard_map(
        functools.partial(body, mesh.shape["blk"]),
        mesh=mesh,
        in_specs=in_specs,
        out_specs=out_specs,
        check_vma=False,
    )
```

time: 115 us -> 36.4 us (0.32)
  Pallas kernels: 0 us -> 30.6 us
  matrix products: 27.5 us -> 0 us
  local copies, waits for them, and re-layouts: 27.6 us -> 3.58 us
  other arithmetic: 21.8 us -> 0.72 us
  between operations: 16.1 us -> 1.29 us
  waiting for transfers between devices: 14.7 us -> 0 us
  starting transfers between devices: 6.61 us -> 0 us
    pallas_call x0 -> x1, Pallas kernels: none -> 30.6 us  [body(): pl.pallas_call(functools.partial(kernel, (nblk, kl, nj, ni, cv)), out_sha...]
    dot_general x4 -> x0, matrix products: 27.5 us -> none  [the longest x3 18.3 us: direction_terms(): jnp.einsum('vw,cwkja->cvkja', jacobian, central, precision=highest)]
    all_gather x1 -> x0, waiting for transfers between devices: 14.7 us -> none  [body(): lax.all_gather(residual, 'line', axis=4, tiled=True)]
    unnamed x22 -> x2, local copies, waits for them, and re-layouts: 16.8 us -> 2.99 us
    sub x1 -> x0, other arithmetic: 11.5 us -> none  [section_residual(): return summed + rotated - source]
    mul x3 -> x1, other arithmetic: 9.17 us -> 0.72 us  [body(): 0.5 * jacobians.reshape(-1)]
    ppermute x2 -> x0, local copies, waits for them, and re-layouts: 6.83 us -> none  [the longest x1 3.41 us: extended(): lax.ppermute(lax.slice_in_dim(block, block.shape[dim] - width, None, axis...]
    ppermute x4 -> x0, starting transfers between devices: 6.58 us -> none  [the longest x2 6.08 us: extended(): lax.ppermute(lax.slice_in_dim(block, 0, width, axis=dim), axis, backward)]
  transfers between devices with their start and end apart: 5 -> 0, of which waited for: 1 -> 0; matrix products, arithmetic and copies ran while one was open for 18% -> 0% of each run, Pallas kernels for 0% -> 0%
where the time goes in v1:
time: 36.4 us; the launch traced here: 36.2 us
  Pallas kernels  30.6 us (84%)
  local copies, waits for them, and re-layouts  3.58 us (10%)
  between operations  1.29 us (4%)
  other arithmetic  0.72 us (2%)
    pallas_call x1, Pallas kernels, body(): pl.pallas_call(functools.partial(kernel, (nblk, kl, nj, ni, cv)), out_sha...  30.6 us
    unnamed x2, local copies, waits for them, and re-layouts  2.99 us

profile of v1, /device:TPU:0, one launch (start us, length us, event | category | flops | bytes accessed | tf_op | source)
XLA Modules:
  0.0 36.2 jit_solution(1202379757076779243)
XLA Ops:
  1.3 0.7 %multiply_reduce_fusion = f32[3,5,5]{2,1,0:T(8,128)S(1)} fusion(f32[1,3,5,5]{3,0,2,1:T(1,128)} %param.11), kind=kLoop, calls=%fused_computation | loop fusion | flops 75 | bytes 600 | tf_op jit(solution)/shard_map/mul | solution.py:367
  2.0 0.6 %mul.10.jac = f32[75]{0:T(128)} reshape(f32[3,5,5]{2,1,0:T(8,128)S(1)} %multiply_reduce_fusion) | data formatting | bytes 600 | tf_op jit(solution)/shard_map/mul | solution.py:367
  2.6 30.6 %shard_map.95 = (f32[10,512,128]{2,1,0:T(8,128)S(1)}, f32[10,512,128]{2,1,0:T(8,128)S(1)}) custom-call(f32[75]{0:T(128)} %mul.10.jac, f32[1]{0:T(128)S(6)} %copy.14.freq, s32[2]{0:T(128)} %bitcast.9, f32[10,32,16,128]{3,2,1,0:T(8,128)} %bitcast.7, f32[10,32,16,128]{3,2,1,0:T(8,128)} %bitcast.8, f32[32,16,128]{2,1,0:T(8,128)} %damp.1, f32[32,16,128]{2,1,0:T(8,128)} %step.1, ...), custom_call_target="tpu_custom_call" | custom-call | tf_op jit(solution)/shard_map/pallas_call | solution.py:338
  33.2 1.5 %copy.12 = f32[2,5,32,16,128]{4,3,2,1,0:T(8,128)} copy(f32[2,5,32,16,128]{4,3,2,1,0:T(8,128)S(1)} %bitcast.6) | data formatting | bytes 5242880
  34.7 1.5 %copy.13 = f32[2,5,32,16,128]{4,3,2,1,0:T(8,128)} copy(f32[2,5,32,16,128]{4,3,2,1,0:T(8,128)S(1)} %bitcast.5) | data formatting | bytes 5242880

commit v2 on v1

--- a/solution.py
+++ b/solution.py
@@ -119,7 +119,7 @@
         )
 
     packed = lax.fori_loop(
-        0, kl, pack, tuple(jnp.zeros((nj, ni), f32) for _ in range(cv))
+        0, kl, pack, tuple(jnp.zeros((nj, ni), f32) for _ in range(cv)), unroll=4
     )
     for n in range(cv):
         pack_out[n] = packed[n]
@@ -143,7 +143,7 @@
         wcat[j, ni : 2 * ni, :] = (values - high.astype(f32)).astype(bf16)
         return carry
 
-    lax.fori_loop(0, nj, split, 0)
+    lax.fori_loop(0, nj, split, 0, unroll=2)
 
     loads[3].wait()
     loads[4].wait()
@@ -177,14 +177,15 @@
                     + 18.0 * u
                 )
             for v in range(nv):
-                total = damping * fourth[v] - gbuf[c * nv + v, k]
+                flux = jnp.zeros((nj, ni), f32)
+                for w in range(nv):
+                    for d in range(3):
+                        flux = flux + jac[d, v, w] * central[w][d]
+                total = damping * fourth[v] - gbuf[c * nv + v, k] + 0.5 * flux
                 if c == 0:
                     total = total - omega * ubuf[nv + v, k + 2, 8 : nj + 8, :]
                 else:
                     total = total + omega * ubuf[v, k + 2, 8 : nj + 8, :]
-                for w in range(nv):
-                    for d in range(3):
-                        total = total + jac[d * nv * nv + v * nv + w] * central[w][d]
                 own[c * nv + v, pl.ds(pl.multiple_of(k * nj, nj), nj), :] = total
 
     def send(pair):
@@ -255,7 +256,7 @@
                     at += count
             return carry
 
-        lax.fori_loop(0, nj, one, 0)
+        lax.fori_loop(0, nj, one, 0, unroll=8)
 
     def update(first, number):
         def one(k, carry):
@@ -267,7 +268,7 @@
                 )
             return carry
 
-        lax.fori_loop(0, number, one, 0)
+        lax.fori_loop(0, number, one, 0, unroll=2)
 
     def arrived(n, carry):
         send(middle_pair(n)).wait_recv()
@@ -284,14 +285,18 @@
         turn = facing[side] == 1
         for p in range(2):
             for n in range(cv):
-                turned[n * 2 + p] = ubuf[n, first + p, 8 : nj + 8, :]
+                at = (p * cv + n) * nj
+                turned[0, at : at + nj, :] = ubuf[n, first + p, 8 : nj + 8, :]
+        for j in range(nj):
+            turned[1, pl.ds(j, 2 * cv, stride=nj), :] = turned[
+                0, pl.ds(nj - 1 - j, 2 * cv, stride=nj), :
+            ]
         for p in range(2):
             for n in range(cv):
                 sign = -1.0 if n % nv == 2 else 1.0
-                rows = [turned[n * 2 + p, r : r + 1, :] for r in range(nj - 1, -1, -1)]
-                flipped = sign * jnp.concatenate(rows, axis=0)
+                at = (p * cv + n) * nj
                 ubuf[n, first + p, 8 : nj + 8, :] = jnp.where(
-                    turn, flipped, turned[n * 2 + p]
+                    turn, sign * turned[1, at : at + nj, :], turned[0, at : at + nj, :]
                 )
 
     work(0)
@@ -351,7 +356,7 @@
             pltpu.VMEM((cv, nj, ni), f32),
             pltpu.VMEM((cv, kl * nj, ni), f32),
             pltpu.VMEM((cv, kl * nj, ni), f32),
-            pltpu.VMEM((cv * 2, nj, ni), f32),
+            pltpu.VMEM((2, cv * 2 * nj, ni), f32),
             dma((6,)),
             dma((2,)),
             dma((2,)),
@@ -364,7 +369,7 @@
             collective_id=0, has_side_effects=True, vmem_limit_bytes=54 * 1024 * 1024
         ),
     )(
-        0.5 * jacobians.reshape(-1),
+        jacobians.reshape(jacobians.shape[1:]),
         frequency,
         orientation.reshape(-1),
         base_state.reshape(cv, kl, nj, ni),

time: 36.4 us -> 29.8 us (0.82)
  Pallas kernels: 30.6 us -> 23.9 us
  other arithmetic: 0.72 us -> 0 us
  local copies, waits for them, and re-layouts: 3.58 us -> 4.29 us
    pallas_call x1, Pallas kernels: 30.6 us -> 23.9 us  [body(): pl.pallas_call(functools.partial(kernel, (nblk, kl, nj, ni, cv)), out_sha...]
    mul x1 -> x0, other arithmetic: 0.72 us -> none  [body(): 0.5 * jacobians.reshape(-1)]
    unnamed x2 -> x3, local copies, waits for them, and re-layouts: 2.99 us -> 3.69 us
    reshape x0 -> x1, local copies, waits for them, and re-layouts: none -> 0.6 us  [body(): jacobians.reshape(jacobians.shape[1:])]
    mul x1 -> x0, local copies, waits for them, and re-layouts: 0.6 us -> none  [body(): 0.5 * jacobians.reshape(-1)]
where the time goes in v2:
time: 29.8 us; the launch traced here: 29.5 us
  Pallas kernels  23.9 us (80%)
  local copies, waits for them, and re-layouts  4.29 us (14%)
  between operations  1.29 us (4%)
    pallas_call x1, Pallas kernels, body(): pl.pallas_call(functools.partial(kernel, (nblk, kl, nj, ni, cv)), out_sha...  23.9 us
    unnamed x3, local copies, waits for them, and re-layouts  3.69 us
    reshape x1, local copies, waits for them, and re-layouts, body(): jacobians.reshape(jacobians.shape[1:])  0.6 us

profile of v2, /device:TPU:0, one launch (start us, length us, event | category | flops | bytes accessed | tf_op | source)
XLA Modules:
  0.0 29.5 jit_solution(1572093283297123085)
XLA Ops:
  1.3 0.7 %copy.13 = f32[1,3,5,5]{3,1,2,0:T(4,128)S(1)} copy(f32[1,3,5,5]{3,0,2,1:T(1,128)} %param.11) | data formatting | bytes 600 | tf_op args[3]
  2.0 0.6 %copy.11.jac = f32[3,5,5]{2,1,0:T(8,128)} copy(f32[3,5,5]{2,0,1:T(4,128)S(1)} %bitcast.12) | data formatting | bytes 600 | tf_op jit(solution)/shard_map/reshape | solution.py:372
  2.6 23.9 %shard_map.95 = (f32[10,512,128]{2,1,0:T(8,128)S(1)}, f32[10,512,128]{2,1,0:T(8,128)S(1)}) custom-call(f32[3,5,5]{2,1,0:T(8,128)} %copy.11.jac, f32[1]{0:T(128)S(6)} %copy.18.freq, s32[2]{0:T(128)} %bitcast.13, f32[10,32,16,128]{3,2,1,0:T(8,128)} %bitcast.10, f32[10,32,16,128]{3,2,1,0:T(8,128)} %bitcast.11, f32[32,16,128]{2,1,0:T(8,128)} %damp.1, ...), custom_call_target="tpu_custom_call" | custom-call | tf_op jit(solution)/shard_map/pallas_call | solution.py:343
  26.5 1.5 %copy.16 = f32[2,5,32,16,128]{4,3,2,1,0:T(8,128)} copy(f32[2,5,32,16,128]{4,3,2,1,0:T(8,128)S(1)} %bitcast.9) | data formatting | bytes 5242880
  28.0 1.5 %copy.17 = f32[2,5,32,16,128]{4,3,2,1,0:T(8,128)} copy(f32[2,5,32,16,128]{4,3,2,1,0:T(8,128)S(1)} %bitcast.8) | data formatting | bytes 5242880

commit v3 on v2

--- a/solution.py
+++ b/solution.py
@@ -10,6 +10,7 @@
 MESH = pl.DeviceIdType.MESH
 section_coefficient = 0.25
 PAIR = 2
+MIXED = 4
 
 
 def kernel(
@@ -225,10 +226,10 @@
         return carry
 
     lax.fori_loop(0, pairs // 2, run_middle, 0)
-    lax.fori_loop(0, 2 * (quarter - 1), run_outer, 0)
-
-    def product(starts, count):
-        def one(j, carry):
+    lax.fori_loop(0, 2 * (quarter - 1) - MIXED, run_outer, 0)
+
+    def row_product(starts, count):
+        def row(j):
             mine, theirs = [], []
             for n in range(cv):
                 for k0 in starts:
@@ -254,6 +255,14 @@
                         at : at + count
                     ]
                     at += count
+
+        return row
+
+    def product(starts, count):
+        row = row_product(starts, count)
+
+        def one(j, carry):
+            row(j)
             return carry
 
         lax.fori_loop(0, nj, one, 0, unroll=8)
@@ -275,7 +284,23 @@
         return carry
 
     lax.fori_loop(0, pairs // 2, arrived, 0)
-    product([kl // 4], kl // 2)
+    middle_row = row_product([kl // 4], kl // 2)
+    each = nj // (MIXED * PAIR)
+
+    def run_mixed(n, carry):
+        pair = outer_pair(n + 2 * (quarter - 1) - MIXED)
+
+        def one(k, inner):
+            for r in range(each):
+                middle_row((n * PAIR + k) * each + r)
+            plane(pair * PAIR + k)
+            return inner
+
+        lax.fori_loop(0, PAIR, one, 0)
+        send(pair).start()
+        return carry
+
+    lax.fori_loop(0, MIXED, run_mixed, 0)
     update(kl // 4, kl // 2)
 
     to_right.wait()
@@ -318,6 +343,25 @@
         return carry
 
     lax.fori_loop(0, pairs, sent, 0)
+
+
+def write_out(advanced, smoothed, advanced_out, smoothed_out, sems):
+    half = advanced.shape[0] // 2
+    copies = []
+    for n, (source, target) in enumerate(
+        ((advanced, advanced_out), (smoothed, smoothed_out))
+    ):
+        for p in range(2):
+            part = pl.ds(p * half, half)
+            copies.append(
+                pltpu.make_async_copy(
+                    source.at[part], target.at[part], sems.at[2 * n + p]
+                )
+            )
+    for copy in copies:
+        copy.start()
+    for copy in copies:
+        copy.wait()
 
 
 def body(
@@ -378,6 +422,18 @@
         time_step,
         line_inverse,
     )
+    shape = jax.ShapeDtypeStruct((cv, kl * nj, ni), f32)
+    advanced, smoothed = pl.pallas_call(
+        write_out,
+        out_shape=(shape, shape),
+        in_specs=[vmem] * 2,
+        out_specs=(hbm, hbm),
+        scratch_shapes=[dma((4,))],
+        compiler_params=pltpu.CompilerParams(vmem_limit_bytes=4 * 1024 * 1024),
+    )(
+        pltpu.with_memory_space_constraint(advanced, pltpu.VMEM),
+        pltpu.with_memory_space_constraint(smoothed, pltpu.VMEM),
+    )
     return advanced.reshape(base_state.shape), smoothed.reshape(base_state.shape)
 
 

time: 29.8 us -> 28.8 us (0.966)
  local copies, waits for them, and re-layouts: 4.29 us -> 1.3 us
  Pallas kernels: 23.9 us -> 26 us
    unnamed x3 -> x1, local copies, waits for them, and re-layouts: 3.69 us -> 0.7 us
    pallas_call x0 -> x1, Pallas kernels: none -> 2.39 us  [body(): pl.pallas_call(write_out, out_shape=(shape, shape), in_specs=[vmem] * 2,...]
    pallas_call x1, Pallas kernels: 23.9 us -> 23.6 us  [body(): pl.pallas_call(functools.partial(kernel, (nblk, kl, nj, ni, cv)), out_sha...]
where the time goes in v3:
time: 28.8 us; the launch traced here: 28.5 us
  Pallas kernels  26 us (90%)
  local copies, waits for them, and re-layouts  1.3 us (5%)
  between operations  1.29 us (4%)
    pallas_call x1, Pallas kernels, body(): pl.pallas_call(functools.partial(kernel, (nblk, kl, nj, ni, cv)), out_sha...  23.6 us
    pallas_call x1, Pallas kernels, body(): pl.pallas_call(write_out, out_shape=(shape, shape), in_specs=[vmem] * 2,...  2.39 us
    unnamed x1, local copies, waits for them, and re-layouts  0.7 us
    reshape x1, local copies, waits for them, and re-layouts, body(): jacobians.reshape(jacobians.shape[1:])  0.6 us

profile of v3, /device:TPU:0, one launch (start us, length us, event | category | flops | bytes accessed | tf_op | source)
XLA Modules:
  0.0 28.5 jit_solution(16429917765728084161)
XLA Ops:
  1.3 0.7 %copy.13 = f32[1,3,5,5]{3,1,2,0:T(4,128)S(1)} copy(f32[1,3,5,5]{3,0,2,1:T(1,128)} %param.11) | data formatting | bytes 600 | tf_op args[3]
  2.0 0.6 %copy.11.jac = f32[3,5,5]{2,1,0:T(8,128)} copy(f32[3,5,5]{2,0,1:T(4,128)S(1)} %bitcast.10) | data formatting | bytes 600 | tf_op jit(solution)/shard_map/reshape | solution.py:416
  2.6 23.6 %shard_map.95 = (f32[10,512,128]{2,1,0:T(8,128)S(1)}, f32[10,512,128]{2,1,0:T(8,128)S(1)}) custom-call(f32[3,5,5]{2,1,0:T(8,128)} %copy.11.jac, f32[1]{0:T(128)S(6)} %copy.14.freq, s32[2]{0:T(128)} %bitcast.11, f32[10,32,16,128]{3,2,1,0:T(8,128)} %bitcast.8, f32[10,32,16,128]{3,2,1,0:T(8,128)} %bitcast.9, f32[32,16,128]{2,1,0:T(8,128)} %damp.1, ...), custom_call_target="tpu_custom_call" | custom-call | tf_op jit(solution)/shard_map/pallas_call | solution.py:387
  26.2 2.4 %shard_map.96 = (f32[10,512,128]{2,1,0:T(8,128)}, f32[10,512,128]{2,1,0:T(8,128)}) custom-call(f32[10,512,128]{2,1,0:T(8,128)S(1)} %get-tuple-element.6.advanced, f32[10,512,128]{2,1,0:T(8,128)S(1)} %get-tuple-element.7.smoothed), custom_call_target="tpu_custom_call" | custom-call | tf_op jit(solution)/shard_map/pallas_call | solution.py:426

commit v4 on v3

--- a/solution.py
+++ b/solution.py
@@ -23,12 +23,11 @@
     damp,
     step,
     inverse,
-    advanced,
     smoothed,
     ubuf,
+    tbuf,
     gbuf,
     dbuf,
-    tbuf,
     wbuf,
     wcat,
     pack_out,
@@ -120,7 +119,7 @@
         )
 
     packed = lax.fori_loop(
-        0, kl, pack, tuple(jnp.zeros((nj, ni), f32) for _ in range(cv)), unroll=4
+        0, kl, pack, tuple(jnp.zeros((nj, ni), f32) for _ in range(cv)), unroll=8
     )
     for n in range(cv):
         pack_out[n] = packed[n]
@@ -265,19 +264,7 @@
             row(j)
             return carry
 
-        lax.fori_loop(0, nj, one, 0, unroll=8)
-
-    def update(first, number):
-        def one(k, carry):
-            rows = pl.ds(pl.multiple_of((first + k) * nj, nj), nj)
-            scale = section_coefficient * tbuf[first + k]
-            for n in range(cv):
-                advanced[n, rows, :] = (
-                    ubuf[n, first + k + 2, 8 : nj + 8, :] - scale * smoothed[n, rows, :]
-                )
-            return carry
-
-        lax.fori_loop(0, number, one, 0, unroll=2)
+        lax.fori_loop(0, nj, one, 0, unroll=16)
 
     def arrived(n, carry):
         send(middle_pair(n)).wait_recv()
@@ -301,7 +288,6 @@
         return carry
 
     lax.fori_loop(0, MIXED, run_mixed, 0)
-    update(kl // 4, kl // 2)
 
     to_right.wait()
     to_left.wait()
@@ -335,8 +321,6 @@
     send(0).wait_recv()
     send(pairs - 1).wait_recv()
     product([0, kl - kl // 4], kl // 4)
-    update(0, kl // 4)
-    update(kl - kl // 4, kl // 4)
 
     def sent(pair, carry):
         send(pair).wait_send()
@@ -345,21 +329,40 @@
     lax.fori_loop(0, pairs, sent, 0)
 
 
-def write_out(advanced, smoothed, advanced_out, smoothed_out, sems):
-    half = advanced.shape[0] // 2
+PARTS = 4
+
+
+def write_out(smoothed, ubuf, tbuf, advanced_out, smoothed_out, abuf, sems):
+    cv, rows_all, _ = smoothed.shape
+    kl, nj, _ = tbuf.shape
     copies = []
-    for n, (source, target) in enumerate(
-        ((advanced, advanced_out), (smoothed, smoothed_out))
-    ):
-        for p in range(2):
-            part = pl.ds(p * half, half)
-            copies.append(
-                pltpu.make_async_copy(
-                    source.at[part], target.at[part], sems.at[2 * n + p]
+    half = cv // 2
+    for p in range(2):
+        part = pl.ds(p * half, half)
+        copies.append(
+            pltpu.make_async_copy(smoothed.at[part], smoothed_out.at[part], sems.at[p])
+        )
+        copies[-1].start()
+    planes = kl // PARTS
+    for p in range(PARTS):
+
+        def one(k, carry):
+            rows = pl.ds(pl.multiple_of(k * nj, nj), nj)
+            scale = section_coefficient * tbuf[k]
+            for n in range(cv):
+                abuf[n, rows, :] = (
+                    ubuf[n, k + 2, 8 : nj + 8, :] - scale * smoothed[n, rows, :]
                 )
+            return carry
+
+        lax.fori_loop(p * planes, (p + 1) * planes, one, 0, unroll=2)
+        part = pl.ds(p * planes * nj, planes * nj)
+        copies.append(
+            pltpu.make_async_copy(
+                abuf.at[:, part], advanced_out.at[:, part], sems.at[2 + p]
             )
-    for copy in copies:
-        copy.start()
+        )
+        copies[-1].start()
     for copy in copies:
         copy.wait()
 
@@ -384,15 +387,17 @@
     hbm = pl.BlockSpec(memory_space=pltpu.HBM)
     vmem = pl.BlockSpec(memory_space=pltpu.VMEM)
     dma = pltpu.SemaphoreType.DMA
-    advanced, smoothed = pl.pallas_call(
+    smoothed, ubuf, tbuf = pl.pallas_call(
         functools.partial(kernel, (nblk, kl, nj, ni, cv)),
-        out_shape=(out, out),
+        out_shape=(
+            out,
+            pltpu.VMEM((cv, kl + 4, nj + 16, ni), f32),
+            pltpu.VMEM((kl, nj, ni), f32),
+        ),
         in_specs=[smem] * 3 + [hbm] * 5,
-        out_specs=(vmem, vmem),
+        out_specs=(vmem,) * 3,
         scratch_shapes=[
-            pltpu.VMEM((cv, kl + 4, nj + 16, ni), f32),
             pltpu.VMEM((cv, kl, nj, ni), f32),
-            pltpu.VMEM((kl, nj, ni), f32),
             pltpu.VMEM((kl, nj, ni), f32),
             pltpu.VMEM((nj, ni, 2 * ni), f32),
             pltpu.VMEM((nj, 2 * ni, 2 * ni), jnp.bfloat16),
@@ -410,7 +415,7 @@
             dma((pairs,)),
         ],
         compiler_params=pltpu.CompilerParams(
-            collective_id=0, has_side_effects=True, vmem_limit_bytes=54 * 1024 * 1024
+            collective_id=0, has_side_effects=True, vmem_limit_bytes=50 * 1024 * 1024
         ),
     )(
         jacobians.reshape(jacobians.shape[1:]),
@@ -426,13 +431,14 @@
     advanced, smoothed = pl.pallas_call(
         write_out,
         out_shape=(shape, shape),
-        in_specs=[vmem] * 2,
+        in_specs=[vmem] * 3,
         out_specs=(hbm, hbm),
-        scratch_shapes=[dma((4,))],
+        scratch_shapes=[pltpu.VMEM((cv, kl * nj, ni), f32), dma((2 + PARTS,))],
         compiler_params=pltpu.CompilerParams(vmem_limit_bytes=4 * 1024 * 1024),
     )(
-        pltpu.with_memory_space_constraint(advanced, pltpu.VMEM),
         pltpu.with_memory_space_constraint(smoothed, pltpu.VMEM),
+        pltpu.with_memory_space_constraint(ubuf, pltpu.VMEM),
+        pltpu.with_memory_space_constraint(tbuf, pltpu.VMEM),
     )
     return advanced.reshape(base_state.shape), smoothed.reshape(base_state.shape)
 

time: 28.8 us -> 28.1 us (0.976)
  Pallas kernels: 26 us -> 25.2 us
    pallas_call x1, Pallas kernels: 23.6 us -> 22.8 us  [body(): pl.pallas_call(functools.partial(kernel, (nblk, kl, nj, ni, cv)), out_sha...]
where the time goes in v4:
time: 28.1 us; the launch traced here: 27.8 us
  Pallas kernels  25.2 us (90%)
  local copies, waits for them, and re-layouts  1.3 us (5%)
  between operations  1.29 us (5%)
    pallas_call x1, Pallas kernels, body(): pl.pallas_call(functools.partial(kernel, (nblk, kl, nj, ni, cv)), out_sha...  22.8 us
    pallas_call x1, Pallas kernels, body(): pl.pallas_call(write_out, out_shape=(shape, shape), in_specs=[vmem] * 3,...  2.4 us
    unnamed x1, local copies, waits for them, and re-layouts  0.7 us
    reshape x1, local copies, waits for them, and re-layouts, body(): jacobians.reshape(jacobians.shape[1:])  0.6 us

profile of v4, /device:TPU:0, one launch (start us, length us, event | category | flops | bytes accessed | tf_op | source)
XLA Modules:
  0.0 27.8 jit_solution(7611930000225808118)
XLA Ops:
  1.3 0.7 %copy.13 = f32[1,3,5,5]{3,1,2,0:T(4,128)S(1)} copy(f32[1,3,5,5]{3,0,2,1:T(1,128)} %param.11) | data formatting | bytes 600 | tf_op args[3]
  2.0 0.6 %copy.11.jac = f32[3,5,5]{2,1,0:T(8,128)} copy(f32[3,5,5]{2,0,1:T(4,128)S(1)} %bitcast.10) | data formatting | bytes 600 | tf_op jit(solution)/shard_map/reshape | solution.py:421
  2.6 22.8 %shard_map.95 = (f32[10,512,128]{2,1,0:T(8,128)S(1)}, f32[10,36,32,128]{3,2,1,0:T(8,128)S(1)}, f32[32,16,128]{2,1,0:T(8,128)S(1)}) custom-call(f32[3,5,5]{2,1,0:T(8,128)} %copy.11.jac, f32[1]{0:T(128)S(6)} %copy.14.freq, s32[2]{0:T(128)} %bitcast.11, f32[10,32,16,128]{3,2,1,0:T(8,128)} %bitcast.8, f32[10,32,16,128]{3,2,1,0:T(8,128)} %bitcast.9, ...), custom_call_target="tpu_custom_call" | custom-call | tf_op jit(solution)/shard_map/pallas_call | solution.py:390
  25.4 2.4 %shard_map.96 = (f32[10,512,128]{2,1,0:T(8,128)}, f32[10,512,128]{2,1,0:T(8,128)}) custom-call(f32[10,512,128]{2,1,0:T(8,128)S(1)} %get-tuple-element.7.smoothed, f32[10,36,32,128]{3,2,1,0:T(8,128)S(1)} %get-tuple-element.8.ubuf, f32[32,16,128]{2,1,0:T(8,128)S(1)} %get-tuple-element.9.tbuf), custom_call_target="tpu_custom_call" | custom-call | tf_op jit(solution)/shard_map/pallas_call | solution.py:431
